TPU v7x, 32 devices: a whole 2x2x4 slice. The times are simulated.
32 devices in a mesh: ctx: 16 (over z, x, core), head: 2 (over y).
Axes of the slice: x: 2, y: 2, z: 4, core: 2. Of those that a mesh axis runs over, the one named last changes fastest.
Arguments:
- queries: bfloat16 [2048, 6144], P('ctx', 'head'), as said below
- keys: bfloat16 [4096, 1024], P('ctx', 'head'), as said below
- values: bfloat16 [4096, 1024], P('ctx', 'head'), may hold values from -6 to 6
- ranges: int32 [4, 2, 2], replicated, may hold values from 0 to 32, as said below
- noise_ids: int32 [4], replicated, may hold values from 0 to 7
- block_position: int32 [32], replicated, may hold values from 0 to 31, as said below
- level_gain: float32 [8, 6144], P(None, 'head'), may hold values from 0.1 to 1.9
Outputs:
- attended: bfloat16 [2048, 6144], P('ctx', 'head')
Inputs may be any that keep to these rules, and one draw needn't show every extreme that they name: block_position is a permutation of 0 to 31. Each range has start < end and spans 1 to 16 blocks; some range spans exactly 16; ranges of a stretch may intersect. `queries`: entries of order one in most rows; a draw may hold a few rows whose entries are up to about 28 times larger. `keys`: entries of order one.
All inputs are finite; a program needn't handle non-finite values.
Results may differ from a plain program's by a relative error of at most 0.0075.
Values may be sent and summed in bfloat16 or wider, within the bound.
No kernel may reach another device: no remote copies, remote signals or barrier semaphores. Data moves between devices by JAX's collectives and lax.ppermute only.
A program may use at most 64 MiB of HBM per device.

v0:
```python
import functools

import jax
import jax.numpy as jnp
from jax import lax
from jax.experimental import pallas as pl
from jax.experimental.pallas import tpu as pltpu
from jax.sharding import PartitionSpec as P

D = 6144
HD = 128
BLK = 128
STRETCHES = 4
LOG2E = 1.4426950408889634
NEGATIVE = -1e30

F32 = jnp.float32
BF16 = jnp.bfloat16
VMEM = pl.BlockSpec(memory_space=pltpu.VMEM)
SMEM = pl.BlockSpec(memory_space=pltpu.SMEM)
ROOM = 52 * 1024 * 1024


def attend_kernel(spec, *refs):
    sources, split, per_device, pieces, group_size, first, last, nr = spec
    where_ref, ranges_ref, position_ref = refs[:3]
    at = 3
    query_refs = refs[at : at + pieces]
    at += pieces
    key_refs, value_refs = refs[at : at + len(sources)], refs[at + len(sources) : at + 2 * len(sources)]
    at += 2 * len(sources)
    if not first:
        acc_in, stat_in = refs[at : at + 2]
        at += 2
    if last:
        out_refs, square_refs = refs[at : at + pieces], refs[at + pieces : at + 2 * pieces]
        at += 2 * pieces
    else:
        acc_out, stat_out = refs[at : at + 2]
        at += 2
    kept_k, kept_v, score_ref, acc_ref = refs[at : at + 4]
    at += 4
    if not first:
        acc_old, stat_old, semaphores = refs[at : at + 3]
        fetches = [
            pltpu.make_async_copy(acc_in, acc_old, semaphores.at[0]),
            pltpu.make_async_copy(stat_in, stat_old, semaphores.at[1]),
        ]
        for fetch in fetches:
            fetch.start()
    q_rows = query_refs[0].shape[0]
    width = pieces * q_rows * group_size
    to_log2 = LOG2E / HD**0.5

    place, stretch, group = where_ref[0], where_ref[1], where_ref[2]
    count = jnp.int32(0)
    for index, bits in enumerate(sources):
        held = jnp.bitwise_xor(group, bits)
        for step in range(split):
            device = held * split + jnp.bitwise_xor(place, step)
            for block in range(per_device):
                logical = position_ref[device * per_device + block]
                live = jnp.bool_(False)
                for r in range(nr):
                    low = ranges_ref[(stretch * nr + r) * 2]
                    high = ranges_ref[(stretch * nr + r) * 2 + 1]
                    live = live | ((logical >= low) & (logical < high))

                @pl.when(live)
                def _(count=count, index=index, slot=step * per_device + block):
                    kept_k[count] = key_refs[index][slot]
                    kept_v[count] = value_refs[index][slot]

                count = count + live.astype(jnp.int32)
    kept_v[count] = jnp.zeros((BLK, HD), BF16)

    pairs = lax.div(count, 2)
    quads = lax.div(count, 4)
    q = jnp.concatenate(
        [ref[:, g * HD : (g + 1) * HD] for ref in query_refs for g in range(group_size)], axis=0
    )
    acc_ref[:, :HD] = jnp.full((width, HD), NEGATIVE, F32)

    def scores(start, blocks):
        keys = kept_k[pl.ds(start, blocks)].reshape(blocks * BLK, HD)
        score = lax.dot_general(q, keys, (((1,), (1,)), ((), ())), preferred_element_type=F32)
        top = score[:, :BLK]
        for b in range(1, blocks):
            top = jnp.maximum(top, score[:, b * BLK : (b + 1) * BLK])
        acc_ref[:, :HD] = jnp.maximum(acc_ref[:, :HD], top)
        return score

    def quad_scores(index, carry):
        score = scores(index * 4, 4)
        score_ref[index * 2] = score[:, : 2 * BLK]
        score_ref[index * 2 + 1] = score[:, 2 * BLK :]
        return carry

    def pair_scores(index, carry):
        score_ref[index] = scores(index * 2, 2)
        return carry

    lax.fori_loop(0, quads, quad_scores, 0)
    lax.fori_loop(quads * 2, pairs, pair_scores, 0)

    @pl.when(count > pairs * 2)
    def _():
        score_ref[pairs, :, :BLK] = scores(count - 1, 1)
        score_ref[pairs, :, BLK:] = jnp.full((width, BLK), NEGATIVE, F32)

    top = jnp.max(acc_ref[:, :HD], axis=1, keepdims=True) * to_log2
    if not first:
        for fetch in fetches:
            fetch.wait()
        old_top = stat_old[:, :1]
        top = jnp.maximum(top, old_top)
        correct = jnp.exp2(old_top - top)
        acc_ref[:, :HD] = acc_old[...] * correct
        acc_ref[:, HD:] = jnp.broadcast_to(stat_old[:, HD // 2 : HD // 2 + 1] * correct, (width, HD))
    else:
        acc_ref[...] = jnp.zeros((width, 2 * HD), F32)
    top_wide = jnp.broadcast_to(top, (width, 2 * BLK))
    ones = jnp.ones((2 * BLK, HD), BF16)

    def sums(index):
        weight = jnp.exp2(score_ref[index] * to_log2 - top_wide).astype(BF16)
        values = jnp.concatenate([kept_v[pl.ds(index * 2, 2)].reshape(2 * BLK, HD), ones], axis=1)
        return jnp.dot(weight, values, preferred_element_type=F32)

    def quad_sums(index, carry):
        acc_ref[...] += sums(index * 2) + sums(index * 2 + 1)
        return carry

    def pair_sums(index, carry):
        acc_ref[...] += sums(index)
        return carry

    steps = lax.div(count + 1, 2)
    twice = lax.div(steps, 2)
    lax.fori_loop(0, twice, quad_sums, 0)
    lax.fori_loop(twice * 2, steps, pair_sums, 0)
    if last:
        heads = acc_ref[:, :HD] / acc_ref[:, HD:]
        for p in range(pieces):
            square = jnp.zeros((q_rows, HD), F32)
            for g in range(group_size):
                start = (p * group_size + g) * q_rows
                part = heads[start : start + q_rows]
                square = square + part * part
                out_refs[p][:, g * HD : (g + 1) * HD] = part.astype(BF16)
            square = jnp.sum(square, axis=1, keepdims=True)
            square_refs[p][...] = jnp.broadcast_to(square, (q_rows, q_rows)).T[:8]
    else:
        acc_out[...] = acc_ref[:, :HD]
        lane = lax.broadcasted_iota(jnp.int32, (width, HD), 1)
        stat_out[...] = jnp.where(lane < HD // 2, jnp.broadcast_to(top, (width, HD)), acc_ref[:, HD:])


def attend(where, ranges, position, q, key_list, value_list, sources, state, last, group_size, per_device):
    pieces = len(q)
    q_rows = q[0].shape[0]
    blocks = key_list[0].shape[0]
    width = pieces * q_rows * group_size
    nr = ranges.shape[0] // (2 * STRETCHES)
    first = state is None
    most = len(sources) * blocks
    spec = (tuple(sources), blocks // per_device, per_device, pieces, group_size, first, last, nr)
    if last:
        shapes = [jax.ShapeDtypeStruct(q[0].shape, BF16)] * pieces + [jax.ShapeDtypeStruct((8, q_rows), F32)] * pieces
    else:
        shapes = [jax.ShapeDtypeStruct((width, HD), F32)] * 2
    inputs = 2 * len(sources) + pieces
    held = [] if first else [pltpu.VMEM((width, HD), F32)] * 2 + [pltpu.SemaphoreType.DMA((2,))]
    return pl.pallas_call(
        functools.partial(attend_kernel, spec),
        in_specs=[SMEM] * 3 + [VMEM] * inputs + [pl.BlockSpec(memory_space=pl.ANY)] * (0 if first else 2),
        out_specs=[VMEM] * len(shapes),
        out_shape=shapes,
        scratch_shapes=[
            pltpu.VMEM((most + 2, BLK, HD), BF16),
            pltpu.VMEM((most + 2, BLK, HD), BF16),
            pltpu.VMEM((most // 2 + 1, width, 2 * BLK), F32),
            pltpu.VMEM((width, 2 * HD), F32),
            *held,
        ],
        compiler_params=pltpu.CompilerParams(vmem_limit_bytes=ROOM),
        cost_estimate=pl.CostEstimate(
            flops=12 * width * most * BLK * HD, bytes_accessed=4 * width * HD, transcendentals=width * most * BLK
        ),
    )(where, ranges, position, *q, *key_list, *value_list, *(() if first else state))


def pieces_kernel(split, where_ref, *refs):
    inputs = len(refs) // (split + 1)
    for index in range(inputs):
        source = refs[index]
        width = source.shape[1] // split
        for step in range(split):
            start = pl.multiple_of(jnp.bitwise_xor(where_ref[0], step) * width, HD)
            refs[inputs + index * split + step][...] = source[:, pl.ds(start, width)]


def pieces_of(where, split, *arrays):
    shapes = []
    for array in arrays:
        shapes += [jax.ShapeDtypeStruct((array.shape[0], array.shape[1] // split), array.dtype)] * split
    out = pl.pallas_call(
        functools.partial(pieces_kernel, split),
        in_specs=[SMEM] + [VMEM] * len(arrays),
        out_specs=[VMEM] * len(shapes),
        out_shape=shapes,
    )(where, *arrays)
    return [out[i * split : (i + 1) * split] for i in range(len(arrays))]


def finish_kernel(split, where_ref, noise_ref, square_ref, gain_ref, *refs):
    out_ref = refs[split]
    q_rows, width = refs[0].shape
    level = noise_ref[where_ref[1]]
    square = jnp.broadcast_to(square_ref[:1], (q_rows, q_rows)).T[:, :1]
    scale = 1.0 / jnp.sqrt(square / D + 1e-06)
    for step in range(split):
        start = pl.multiple_of(jnp.bitwise_xor(where_ref[0], step) * width, HD)
        gain = gain_ref[pl.ds(level, 1), pl.ds(start, width)]
        out_ref[:, pl.ds(start, width)] = (refs[step][...].astype(F32) * scale * gain).astype(BF16)


def body(queries, keys, values, ranges, noise_ids, block_position, level_gain):
    devices = lax.axis_size("ctx")
    q_rows = queries.shape[0]
    heads_here = keys.shape[1] // HD
    group_size = queries.shape[1] // keys.shape[1]
    per_device = keys.shape[0] // BLK
    stretch_devices = devices // STRETCHES
    shared = heads_here == stretch_devices and heads_here & (heads_here - 1) == 0 and STRETCHES & (STRETCHES - 1) == 0
    split = heads_here if shared else 1
    groups = devices // split
    me = lax.axis_index("ctx")
    here = jnp.stack([lax.rem(me, split), lax.div(me, stretch_devices), lax.div(me, split)]).astype(jnp.int32)
    ranges_flat = ranges.reshape(-1)

    def permute(array, pairs):
        return lax.ppermute(array, "ctx", pairs)

    def within(step):
        return [(i, i ^ step) for i in range(devices)]

    def between(bits):
        return [(i, (i // split ^ bits) * split + i % split) for i in range(devices)]

    if shared:
        key_pieces, value_pieces = pieces_of(here, split, keys, values)
        (query_pieces,) = pieces_of(here, split, queries)
        own = []
        for pieces in (key_pieces, value_pieces):
            got = [pieces[0]] + [permute(pieces[step], within(step)) for step in range(1, split)]
            own.append(jnp.concatenate(got, axis=0).reshape(split * per_device, BLK, HD))
        q = [query_pieces[0]] + [permute(query_pieces[step], within(step)) for step in range(1, split)]
        have = [(0, own)]
        reach = groups
        while reach > 1:
            have += [(bits ^ (reach - 1), [permute(array, between(reach - 1)) for array in rows]) for bits, rows in have]
            reach //= 2
        phases = [have[:1], have[1:-1], have[-1:]]
        state = None
        for index, phase in enumerate(phases):
            state = attend(
                here, ranges_flat, block_position, q, [rows[0] for _, rows in phase], [rows[1] for _, rows in phase],
                [bits for bits, _ in phase], state, index == len(phases) - 1, group_size, per_device,
            )
        outs, squares = state[:split], state[split:]
        square = squares[0]
        for step in range(1, split):
            square = square + permute(squares[step], within(step))
        outs = [outs[0]] + [permute(outs[step], within(step)) for step in range(1, split)]
    else:
        key_all = lax.all_gather(keys, "ctx", axis=0, tiled=True)
        value_all = lax.all_gather(values, "ctx", axis=0, tiled=True)
        chunk = min(32, key_all.shape[0] // BLK)
        outs, square = [], 0.0
        for head in range(heads_here):
            columns = slice(head * HD, (head + 1) * HD)
            q = [queries[:, head * group_size * HD : (head + 1) * group_size * HD]]
            head_keys = key_all[:, columns].reshape(-1, chunk, BLK, HD)
            head_values = value_all[:, columns].reshape(-1, chunk, BLK, HD)
            state, chunks = None, head_keys.shape[0]
            for index in range(chunks):
                numbers = jnp.stack([jnp.int32(0), here[1], jnp.int32(0)])
                state = attend(
                    numbers, ranges_flat, block_position, q, [head_keys[index]], [head_values[index]],
                    [index], state, index == chunks - 1, group_size, chunk,
                )
            outs.append(state[0])
            square = square + state[1]
        outs = [jnp.concatenate(outs, axis=1)]
    square = lax.psum(square, "head")
    return pl.pallas_call(
        functools.partial(finish_kernel, split),
        in_specs=[SMEM, SMEM] + [VMEM] * (2 + split),
        out_specs=VMEM,
        out_shape=jax.ShapeDtypeStruct(queries.shape, BF16),
    )(here, noise_ids, square, level_gain, *outs)


def solution(mesh):
    placed = (P("ctx", "head"), P("ctx", "head"), P("ctx", "head"), P(), P(), P(), P(None, "head"))
    return jax.shard_map(
        body, mesh=mesh, in_specs=placed, out_specs=P("ctx", "head"), check_vma=False
    )
```

profile of v0, /device:TPU:27, one launch (start us, length us, event | category | flops | bytes accessed | tf_op | source)
XLA Modules:
  0.0 77.7 jit_solution(6896023837454501544)
XLA Ops:
  0.0 0.6 pad_add_fusion.where_ref.refs_0_
  0.6 1.9 %shard_map.74 = (bf16[256,128]{1,0:T(8,128)(2,1)}, bf16[256,128]{1,0:T(8,128)(2,1)}, bf16[256,128]{1,0:T(8,128)(2,1)}, bf16[256,128]{1,0:T(8,128)(2,1)}, bf16[25...) custom-call(s32[3]{0:T(128)} %pad_add_fusion.where_ref.refs_0_, ...), custom_call_target="tpu_custom_call" | custom-call | tf_op jit(solution)/shard_map/pallas_call | solution.py:207
  2.6 0.8 %collective-permute-start.10 = (bf16[256,128]{1,0:T(8,128)(2,1)}, bf16[256,128]{1,0:T(8,128)(2,1)S(1)}, u32[]{:S(2)}, u32[]{:S(2)}) collective-permute-start(bf16[256,128]{1,0:T(8,128)(2,1)} %get-tuple-element.40), channel_id=1, source_target_pairs={{0,6},{2,4},{4,2},{6,0},{8,14},{10,12},{12,10},{14,8},{16,22},{18,... | collective-permute-start | bytes 196616 | tf_op jit(solution)/shard_map/ppermute | solution.py:243
  3.4 1.2 %collective-permute-start.9 = (bf16[256,128]{1,0:T(8,128)(2,1)}, bf16[256,128]{1,0:T(8,128)(2,1)S(1)}, u32[]{:S(2)}, u32[]{:S(2)}) collective-permute-start(bf16[256,128]{1,0:T(8,128)(2,1)} %get-tuple-element.39), channel_id=1, source_target_pairs={{0,4},{2,6},{4,0},{6,2},{8,12},{10,14},{12,8},{14,10},{16,20},{18,... | collective-permute-start | bytes 196616 | tf_op jit(solution)/shard_map/ppermute | solution.py:243
  4.6 0.8 %collective-permute-start.3 = (bf16[256,128]{1,0:T(8,128)(2,1)}, bf16[256,128]{1,0:T(8,128)(2,1)S(1)}, u32[]{:S(2)}, u32[]{:S(2)}) collective-permute-start(bf16[256,128]{1,0:T(8,128)(2,1)} %get-tuple-element.34), channel_id=1, source_target_pairs={{0,2},{2,0},{4,6},{6,4},{8,10},{10,8},{12,14},{14,12},{16,18},{18,... | collective-permute-start | bytes 196616 | tf_op jit(solution)/shard_map/ppermute | solution.py:243
  5.4 0.3 collective-permute-start.4
  5.6 2.1 %shard_map.73 = (bf16[128,768]{1,0:T(8,128)(2,1)}, bf16[128,768]{1,0:T(8,128)(2,1)}, bf16[128,768]{1,0:T(8,128)(2,1)}, bf16[128,768]{1,0:T(8,128)(2,1)}) custom-call(s32[3]{0:T(128)} %pad_add_fusion.where_ref.refs_0_, bf16[128,3072]{1,0:T(8,128)(2,1)} %refs_0_.2), custom_call_target="tpu_custom_call" | custom-call | tf_op jit(solution)/shard_map/pallas_call | solution.py:207
  7.7 0.8 copy.9
  8.6 1.4 %collective-permute-start.5 = (bf16[256,128]{1,0:T(8,128)(2,1)}, bf16[256,128]{1,0:T(8,128)(2,1)S(1)}, u32[]{:S(2)}, u32[]{:S(2)}) collective-permute-start(bf16[256,128]{1,0:T(8,128)(2,1)} %get-tuple-element.36), channel_id=1, source_target_pairs={{0,6},{2,4},{4,2},{6,0},{8,14},{10,12},{12,10},{14,8},{16,22},{18,... | collective-permute-start | bytes 196616 | tf_op jit(solution)/shard_map/ppermute | solution.py:243
  10.3 0.3 collective-permute-start.1
  10.5 1.7 %collective-permute-start.2 = (bf16[128,768]{1,0:T(8,128)(2,1)}, bf16[128,768]{1,0:T(8,128)(2,1)S(1)}, u32[]{:S(2)}, u32[]{:S(2)}) collective-permute-start(bf16[128,768]{1,0:T(8,128)(2,1)} %get-tuple-element.32), channel_id=1, source_target_pairs={{0,6},{2,4},{4,2},{6,0},{8,14},{10,12},{12,10},{14,8},{16,22},{18,... | collective-permute-start | bytes 589832 | tf_op jit(solution)/shard_map/ppermute | solution.py:243
  12.2 0.9 %pad_maximum_fusion.1 = bf16[1024,128]{1,0:T(8,128)(2,1)S(1)} fusion(bf16[256,128]{1,0:T(8,128)(2,1)S(1)} %collective-permute-done.10, bf16[256,128]{1,0:T(8,128)(2,1)S(1)} %collective-permute-done.9, bf16[256,128]{1,0:T(8,128)(2,1)S(1)} %collective-permute-done.8, bf16[256,128]{1,0:T(8,128)(2,1)} %get-tuple-element.37), kind=kLoop, calls=%fused_computation.1 | loop fusion | flops 1048576 | bytes 524288 | tf_op jit(solution)/shard_map/concatenate | solution.py:257
  13.1 0.3 collective-permute-start.14
  13.5 0.9 %pad_maximum_fusion = bf16[1024,128]{1,0:T(8,128)(2,1)S(1)} fusion(bf16[256,128]{1,0:T(8,128)(2,1)S(1)} %collective-permute-done.5, bf16[256,128]{1,0:T(8,128)(2,1)S(1)} %collective-permute-done.4, bf16[256,128]{1,0:T(8,128)(2,1)S(1)} %collective-permute-done.3, bf16[256,128]{1,0:T(8,128)(2,1)} %get-tuple-element.33), kind=kLoop, calls=%fused_computation | loop fusion | flops 1048576 | bytes 524288 | tf_op jit(solution)/shard_map/concatenate | solution.py:257
  14.3 1.3 %collective-permute-start.13 = (bf16[8,128,128]{2,1,0:T(8,128)(2,1)S(1)}, bf16[8,128,128]{2,1,0:T(8,128)(2,1)S(1)}, u32[]{:S(2)}, u32[]{:S(2)}) collective-permute-start(bf16[8,128,128]{2,1,0:T(8,128)(2,1)S(1)} %bitcast.7), channel_id=1, source_target_pairs={{0,8},{2,10},{4,12},{6,14},{8,0},{10,2},{12,4},{14,6},{16,24},{18,... | collective-permute-start | bytes 786440 | tf_op jit(solution)/shard_map/ppermute | solution.py:243
  15.6 1.1 %collective-permute-done.1.refs_5_ = bf16[128,768]{1,0:T(8,128)(2,1)S(1)} collective-permute-done((bf16[128,768]{1,0:T(8,128)(2,1)}, bf16[128,768]{1,0:T(8,128)(2,1)S(1)}, u32[]{:S(2)}, u32[]{:S(2)}) %collective-permute-start.1) | collective-permute-done | bytes 196640 | tf_op jit(solution)/shard_map/ppermute | solution.py:243
  16.7 2.1 %collective-permute-start.6 = (bf16[8,128,128]{2,1,0:T(8,128)(2,1)S(1)}, bf16[8,128,128]{2,1,0:T(8,128)(2,1)S(1)}, u32[]{:S(2)}, u32[]{:S(2)}) collective-permute-start(bf16[8,128,128]{2,1,0:T(8,128)(2,1)S(1)} %bitcast.8), channel_id=1, source_target_pairs={{0,24},{2,26},{4,28},{6,30},{8,16},{10,18},{12,20},{14,22},{16,8},... | collective-permute-start | bytes 786440 | tf_op jit(solution)/shard_map/ppermute | solution.py:243
  18.8 2.8 %collective-permute-done.2.refs_6_ = bf16[128,768]{1,0:T(8,128)(2,1)S(1)} collective-permute-done((bf16[128,768]{1,0:T(8,128)(2,1)}, bf16[128,768]{1,0:T(8,128)(2,1)S(1)}, u32[]{:S(2)}, u32[]{:S(2)}) %collective-permute-start.2) | collective-permute-done | bytes 196640 | tf_op jit(solution)/shard_map/ppermute | solution.py:243
  21.6 0.9 %copy-done.2 = bf16[128,768]{1,0:T(8,128)(2,1)S(1)} copy-done((bf16[128,768]{1,0:T(8,128)(2,1)S(1)}, bf16[128,768]{1,0:T(8,128)(2,1)}, u32[]{:S(2)}) %copy-start.2) | copy-done | bytes 196632
  22.5 7.7 %shard_map.75 = (f32[3072,128]{1,0:T(8,128)}, f32[3072,128]{1,0:T(8,128)}) custom-call(s32[3]{0:T(128)S(1)} %copy-done.1, s32[16]{0:T(128)S(1)} %reshape.9.refs_1_, s32[32]{0:T(128)S(1)} %copy-done.4, bf16[128,768]{1,0:T(8,128)(2,1)S(1)} %copy-done.2, bf16[128,768]{1,0:T(8,128)(2,1)S(1)} %collective-permute-done.refs_4_, ...), custom_call_target="tpu_custom_call" | custom-call | flops 4831838208 | bytes 1572864 | tf_op jit(solution)/shard_map/pallas_call | solution.py:174
  30.3 9.5 %collective-permute-done.6.refs_7_ = bf16[8,128,128]{2,1,0:T(8,128)(2,1)S(1)} collective-permute-done((bf16[8,128,128]{2,1,0:T(8,128)(2,1)S(1)}, bf16[8,128,128]{2,1,0:T(8,128)(2,1)S(1)}, u32[]{:S(2)}, u32[]{:S(2)}) %collective-permute-start.6) | collective-permute-done | bytes 262176 | tf_op jit(solution)/shard_map/ppermute | solution.py:243
  39.8 11.3 %shard_map.76 = (f32[3072,128]{1,0:T(8,128)}, f32[3072,128]{1,0:T(8,128)}) custom-call(s32[3]{0:T(128)S(1)} %copy-done.1, s32[16]{0:T(128)S(1)} %reshape.9.refs_1_, s32[32]{0:T(128)S(1)} %copy-done.4, bf16[128,768]{1,0:T(8,128)(2,1)S(1)} %copy-done.2, bf16[128,768]{1,0:T(8,128)(2,1)S(1)} %collective-permute-done.refs_4_, ...), custom_call_target="tpu_custom_call" | custom-call | flops 9663676416 | bytes 1572864 | tf_op jit(solution)/shard_map/pallas_call | solution.py:174
  51.2 0.7 copy-done.8
  51.9 8.2 %shard_map.77 = (bf16[128,768]{1,0:T(8,128)(2,1)S(1)}, bf16[128,768]{1,0:T(8,128)(2,1)S(1)}, bf16[128,768]{1,0:T(8,128)(2,1)S(1)}, bf16[128,768]{1,0:T(8,128)(2,...) custom-call(s32[3]{0:T(128)S(1)} %copy-done.1, ...), custom_call_target="tpu_custom_call" | custom-call | flops 4831838208 | bytes 1572864 | tf_op jit(solution)/shard_map/pallas_call | solution.py:174
  60.1 0.7 copy-done
  60.8 1.0 %collective-permute-start.15 = (f32[8,128]{1,0:T(8,128)S(1)}, f32[8,128]{1,0:T(8,128)S(1)}, u32[]{:S(2)}, u32[]{:S(2)}) collective-permute-start(f32[8,128]{1,0:T(8,128)S(1)} %get-tuple-element.46), channel_id=1, source_target_pairs={{0,2},{2,0},{4,6},{6,4},{8,10},{10,8},{12,14},{14,12},{16,18},{18,... | collective-permute-start | bytes 12296 | tf_op jit(solution)/shard_map/ppermute | solution.py:243
  62.0 1.4 %collective-permute-start.17 = (f32[8,128]{1,0:T(8,128)S(1)}, f32[8,128]{1,0:T(8,128)S(1)}, u32[]{:S(2)}, u32[]{:S(2)}) collective-permute-start(f32[8,128]{1,0:T(8,128)S(1)} %get-tuple-element.48), channel_id=1, source_target_pairs={{0,6},{2,4},{4,2},{6,0},{8,14},{10,12},{12,10},{14,8},{16,22},{18,... | collective-permute-start | bytes 12296 | tf_op jit(solution)/shard_map/ppermute | solution.py:243
  63.9 1.7 %collective-permute-start.20 = (bf16[128,768]{1,0:T(8,128)(2,1)S(1)}, bf16[128,768]{1,0:T(8,128)(2,1)S(1)}, u32[]{:S(2)}, u32[]{:S(2)}) collective-permute-start(bf16[128,768]{1,0:T(8,128)(2,1)S(1)} %get-tuple-element.52), channel_id=1, source_target_pairs={{0,6},{2,4},{4,2},{6,0},{8,14},{10,12},{12,10},{14,8},{16,22},{18,... | collective-permute-start | bytes 589832 | tf_op jit(solution)/shard_map/ppermute | solution.py:243
  65.6 4.7 %psum.7.square_ref = f32[8,128]{1,0:T(8,128)} all-reduce(f32[8,128]{1,0:T(8,128)S(1)} %add_add_fusion), channel_id=1, replica_groups=mesh['ctx'=16,'head'=2] {'head'}, use_global_device_ids=true, to_apply=%region_0.0 | all-reduce | flops 1024 | bytes 8192 | tf_op jit(solution)/shard_map/psum | solution.py:296
  70.3 4.2 %collective-permute-done.20.refs_3_ = bf16[128,768]{1,0:T(8,128)(2,1)S(1)} collective-permute-done((bf16[128,768]{1,0:T(8,128)(2,1)S(1)}, bf16[128,768]{1,0:T(8,128)(2,1)S(1)}, u32[]{:S(2)}, u32[]{:S(2)}) %collective-permute-start.20) | collective-permute-done | bytes 196640 | tf_op jit(solution)/shard_map/ppermute | solution.py:243
  74.5 0.7 copy-done.7
  75.2 2.5 %shard_map.78 = bf16[128,3072]{1,0:T(8,128)(2,1)} custom-call(s32[3]{0:T(128)} %pad_add_fusion.where_ref.refs_0_, s32[4]{0:T(128)} %noise_ref.1, f32[8,128]{1,0:T(8,128)} %psum.7.square_ref, f32[8,3072]{1,0:T(8,128)} %gain_ref.1, bf16[128,768]{1,0:T(8,128)(2,1)} %copy-done, bf16[128,768]{1,0:T(8,128)(2,1)} %copy-done.5, bf16[128,768]{1,0:T(8,128)(2,1)} %copy-done.6, ...), custom_call_target="tpu_custom_call" | custom-call | tf_op jit(solution)/shard_map/pallas_call | solution.py:297
  (41 shorter events, 1.2 us)
Async XLA Ops:
  0.0 21.6 %copy-start.4 = (s32[32]{0:T(128)S(1)}, s32[32]{0:T(128)}, u32[]{:S(2)}) copy-start(s32[32]{0:T(128)} %refs_2_.5) | copy-start | bytes 388
  0.6 21.0 %copy-start.1 = (s32[3]{0:T(128)S(1)}, s32[3]{0:T(128)}, u32[]{:S(2)}) copy-start(s32[3]{0:T(128)} %pad_add_fusion.where_ref.refs_0_) | copy-start | bytes 40
  2.6 6.0 %collective-permute-start.10 = (bf16[256,128]{1,0:T(8,128)(2,1)}, bf16[256,128]{1,0:T(8,128)(2,1)S(1)}, u32[]{:S(2)}, u32[]{:S(2)}) collective-permute-start(bf16[256,128]{1,0:T(8,128)(2,1)} %get-tuple-element.40), channel_id=1, source_target_pairs={{0,6},{2,4},{4,2},{6,0},{8,14},{10,12},{12,10},{14,8},{16,22},{18,... | collective-permute-start | bytes 196616 | tf_op jit(solution)/shard_map/ppermute | solution.py:243
  3.4 6.6 %collective-permute-start.8 = (bf16[256,128]{1,0:T(8,128)(2,1)}, bf16[256,128]{1,0:T(8,128)(2,1)S(1)}, u32[]{:S(2)}, u32[]{:S(2)}) collective-permute-start(bf16[256,128]{1,0:T(8,128)(2,1)} %get-tuple-element.38), channel_id=1, source_target_pairs={{0,2},{2,0},{4,6},{6,4},{8,10},{10,8},{12,14},{14,12},{16,18},{18,... | collective-permute-start | bytes 196616 | tf_op jit(solution)/shard_map/ppermute | solution.py:243
  3.4 6.9 %collective-permute-start.9 = (bf16[256,128]{1,0:T(8,128)(2,1)}, bf16[256,128]{1,0:T(8,128)(2,1)S(1)}, u32[]{:S(2)}, u32[]{:S(2)}) collective-permute-start(bf16[256,128]{1,0:T(8,128)(2,1)} %get-tuple-element.39), channel_id=1, source_target_pairs={{0,4},{2,6},{4,0},{6,2},{8,12},{10,14},{12,8},{14,10},{16,20},{18,... | collective-permute-start | bytes 196616 | tf_op jit(solution)/shard_map/ppermute | solution.py:243
  4.6 5.9 %collective-permute-start.3 = (bf16[256,128]{1,0:T(8,128)(2,1)}, bf16[256,128]{1,0:T(8,128)(2,1)S(1)}, u32[]{:S(2)}, u32[]{:S(2)}) collective-permute-start(bf16[256,128]{1,0:T(8,128)(2,1)} %get-tuple-element.34), channel_id=1, source_target_pairs={{0,2},{2,0},{4,6},{6,4},{8,10},{10,8},{12,14},{14,12},{16,18},{18,... | collective-permute-start | bytes 196616 | tf_op jit(solution)/shard_map/ppermute | solution.py:243
  5.4 7.7 %collective-permute-start.4 = (bf16[256,128]{1,0:T(8,128)(2,1)}, bf16[256,128]{1,0:T(8,128)(2,1)S(1)}, u32[]{:S(2)}, u32[]{:S(2)}) collective-permute-start(bf16[256,128]{1,0:T(8,128)(2,1)} %get-tuple-element.35), channel_id=1, source_target_pairs={{0,4},{2,6},{4,0},{6,2},{8,12},{10,14},{12,8},{14,10},{16,20},{18,... | collective-permute-start | bytes 196616 | tf_op jit(solution)/shard_map/ppermute | solution.py:243
  8.6 4.5 %collective-permute-start.5 = (bf16[256,128]{1,0:T(8,128)(2,1)}, bf16[256,128]{1,0:T(8,128)(2,1)S(1)}, u32[]{:S(2)}, u32[]{:S(2)}) collective-permute-start(bf16[256,128]{1,0:T(8,128)(2,1)} %get-tuple-element.36), channel_id=1, source_target_pairs={{0,6},{2,4},{4,2},{6,0},{8,14},{10,12},{12,10},{14,8},{16,22},{18,... | collective-permute-start | bytes 196616 | tf_op jit(solution)/shard_map/ppermute | solution.py:243
  10.0 4.3 %collective-permute-start = (bf16[128,768]{1,0:T(8,128)(2,1)}, bf16[128,768]{1,0:T(8,128)(2,1)S(1)}, u32[]{:S(2)}, u32[]{:S(2)}) collective-permute-start(bf16[128,768]{1,0:T(8,128)(2,1)} %get-tuple-element.30), channel_id=1, source_target_pairs={{0,2},{2,0},{4,6},{6,4},{8,10},{10,8},{12,14},{14,12},{16,18},{18,... | collective-permute-start | bytes 589832 | tf_op jit(solution)/shard_map/ppermute | solution.py:243
  10.3 6.4 %collective-permute-start.1 = (bf16[128,768]{1,0:T(8,128)(2,1)}, bf16[128,768]{1,0:T(8,128)(2,1)S(1)}, u32[]{:S(2)}, u32[]{:S(2)}) collective-permute-start(bf16[128,768]{1,0:T(8,128)(2,1)} %get-tuple-element.31), channel_id=1, source_target_pairs={{0,4},{2,6},{4,0},{6,2},{8,12},{10,14},{12,8},{14,10},{16,20},{18,... | collective-permute-start | bytes 589832 | tf_op jit(solution)/shard_map/ppermute | solution.py:243
  10.5 11.1 %collective-permute-start.2 = (bf16[128,768]{1,0:T(8,128)(2,1)}, bf16[128,768]{1,0:T(8,128)(2,1)S(1)}, u32[]{:S(2)}, u32[]{:S(2)}) collective-permute-start(bf16[128,768]{1,0:T(8,128)(2,1)} %get-tuple-element.32), channel_id=1, source_target_pairs={{0,6},{2,4},{4,2},{6,0},{8,14},{10,12},{12,10},{14,8},{16,22},{18,... | collective-permute-start | bytes 589832 | tf_op jit(solution)/shard_map/ppermute | solution.py:243
  13.0 17.2 %collective-permute-start.11 = (bf16[8,128,128]{2,1,0:T(8,128)(2,1)S(1)}, bf16[8,128,128]{2,1,0:T(8,128)(2,1)S(1)}, u32[]{:S(2)}, u32[]{:S(2)}) collective-permute-start(bf16[8,128,128]{2,1,0:T(8,128)(2,1)S(1)} %bitcast.4), channel_id=1, source_target_pairs={{0,24},{2,26},{4,28},{6,30},{8,16},{10,18},{12,20},{14,22},{16,8},... | collective-permute-start | bytes 786440 | tf_op jit(solution)/shard_map/ppermute | solution.py:243
  13.1 26.7 %collective-permute-start.14 = (bf16[8,128,128]{2,1,0:T(8,128)(2,1)S(1)}, bf16[8,128,128]{2,1,0:T(8,128)(2,1)S(1)}, u32[]{:S(2)}, u32[]{:S(2)}) collective-permute-start(bf16[8,128,128]{2,1,0:T(8,128)(2,1)S(1)} %bitcast.5), channel_id=1, source_target_pairs={{0,8},{2,10},{4,12},{6,14},{8,0},{10,2},{12,4},{14,6},{16,24},{18,... | collective-permute-start | bytes 786440 | tf_op jit(solution)/shard_map/ppermute | solution.py:243
  14.3 25.5 %collective-permute-start.13 = (bf16[8,128,128]{2,1,0:T(8,128)(2,1)S(1)}, bf16[8,128,128]{2,1,0:T(8,128)(2,1)S(1)}, u32[]{:S(2)}, u32[]{:S(2)}) collective-permute-start(bf16[8,128,128]{2,1,0:T(8,128)(2,1)S(1)} %bitcast.7), channel_id=1, source_target_pairs={{0,8},{2,10},{4,12},{6,14},{8,0},{10,2},{12,4},{14,6},{16,24},{18,... | collective-permute-start | bytes 786440 | tf_op jit(solution)/shard_map/ppermute | solution.py:243
  16.7 23.1 %collective-permute-start.6 = (bf16[8,128,128]{2,1,0:T(8,128)(2,1)S(1)}, bf16[8,128,128]{2,1,0:T(8,128)(2,1)S(1)}, u32[]{:S(2)}, u32[]{:S(2)}) collective-permute-start(bf16[8,128,128]{2,1,0:T(8,128)(2,1)S(1)} %bitcast.8), channel_id=1, source_target_pairs={{0,24},{2,26},{4,28},{6,30},{8,16},{10,18},{12,20},{14,22},{16,8},... | collective-permute-start | bytes 786440 | tf_op jit(solution)/shard_map/ppermute | solution.py:243
  21.6 0.9 %copy-start.2 = (bf16[128,768]{1,0:T(8,128)(2,1)S(1)}, bf16[128,768]{1,0:T(8,128)(2,1)}, u32[]{:S(2)}) copy-start(bf16[128,768]{1,0:T(8,128)(2,1)} %get-tuple-element.29.refs_3_) | copy-start | bytes 589828
  30.3 20.9 %collective-permute-start.12 = (bf16[8,128,128]{2,1,0:T(8,128)(2,1)S(1)}, bf16[8,128,128]{2,1,0:T(8,128)(2,1)S(1)}, u32[]{:S(2)}, u32[]{:S(2)}) collective-permute-start(bf16[8,128,128]{2,1,0:T(8,128)(2,1)S(1)} %collective-permute-done.11.refs_9_), channel_id=1, source_target_pairs={{0,8},{2,10},{4,12},{6,14},{8,0},{10,2},{12,4},{14,6},{16,24},{18,... | collective-permute-start | bytes 786440 | tf_op jit(solution)/shard_map/ppermute | solution.py:243
  39.8 11.4 %collective-permute-start.7 = (bf16[8,128,128]{2,1,0:T(8,128)(2,1)S(1)}, bf16[8,128,128]{2,1,0:T(8,128)(2,1)S(1)}, u32[]{:S(2)}, u32[]{:S(2)}) collective-permute-start(bf16[8,128,128]{2,1,0:T(8,128)(2,1)S(1)} %collective-permute-done.6.refs_7_), channel_id=1, source_target_pairs={{0,8},{2,10},{4,12},{6,14},{8,0},{10,2},{12,4},{14,6},{16,24},{18,... | collective-permute-start | bytes 786440 | tf_op jit(solution)/shard_map/ppermute | solution.py:243
  39.8 12.1 %copy-start.3 = (bf16[128,768]{1,0:T(8,128)(2,1)S(1)}, bf16[128,768]{1,0:T(8,128)(2,1)}, u32[]{:S(2)}) copy-start(bf16[128,768]{1,0:T(8,128)(2,1)} %get-tuple-element.29.refs_3_) | copy-start | bytes 589828
  51.2 0.7 copy-start.8
  60.1 0.7 copy-start
  60.8 3.2 %collective-permute-start.15 = (f32[8,128]{1,0:T(8,128)S(1)}, f32[8,128]{1,0:T(8,128)S(1)}, u32[]{:S(2)}, u32[]{:S(2)}) collective-permute-start(f32[8,128]{1,0:T(8,128)S(1)} %get-tuple-element.46), channel_id=1, source_target_pairs={{0,2},{2,0},{4,6},{6,4},{8,10},{10,8},{12,14},{14,12},{16,18},{18,... | collective-permute-start | bytes 12296 | tf_op jit(solution)/shard_map/ppermute | solution.py:243
  61.8 3.8 %collective-permute-start.16 = (f32[8,128]{1,0:T(8,128)S(1)}, f32[8,128]{1,0:T(8,128)S(1)}, u32[]{:S(2)}, u32[]{:S(2)}) collective-permute-start(f32[8,128]{1,0:T(8,128)S(1)} %get-tuple-element.47), channel_id=1, source_target_pairs={{0,4},{2,6},{4,0},{6,2},{8,12},{10,14},{12,8},{14,10},{16,20},{18,... | collective-permute-start | bytes 12296 | tf_op jit(solution)/shard_map/ppermute | solution.py:243
  62.0 3.5 %collective-permute-start.17 = (f32[8,128]{1,0:T(8,128)S(1)}, f32[8,128]{1,0:T(8,128)S(1)}, u32[]{:S(2)}, u32[]{:S(2)}) collective-permute-start(f32[8,128]{1,0:T(8,128)S(1)} %get-tuple-element.48), channel_id=1, source_target_pairs={{0,6},{2,4},{4,2},{6,0},{8,14},{10,12},{12,10},{14,8},{16,22},{18,... | collective-permute-start | bytes 12296 | tf_op jit(solution)/shard_map/ppermute | solution.py:243
  63.4 6.8 %collective-permute-start.18 = (bf16[128,768]{1,0:T(8,128)(2,1)S(1)}, bf16[128,768]{1,0:T(8,128)(2,1)S(1)}, u32[]{:S(2)}, u32[]{:S(2)}) collective-permute-start(bf16[128,768]{1,0:T(8,128)(2,1)S(1)} %get-tuple-element.50), channel_id=1, source_target_pairs={{0,2},{2,0},{4,6},{6,4},{8,10},{10,8},{12,14},{14,12},{16,18},{18,... | collective-permute-start | bytes 589832 | tf_op jit(solution)/shard_map/ppermute | solution.py:243
  63.7 6.6 %collective-permute-start.19 = (bf16[128,768]{1,0:T(8,128)(2,1)S(1)}, bf16[128,768]{1,0:T(8,128)(2,1)S(1)}, u32[]{:S(2)}, u32[]{:S(2)}) collective-permute-start(bf16[128,768]{1,0:T(8,128)(2,1)S(1)} %get-tuple-element.51), channel_id=1, source_target_pairs={{0,4},{2,6},{4,0},{6,2},{8,12},{10,14},{12,8},{14,10},{16,20},{18,... | collective-permute-start | bytes 589832 | tf_op jit(solution)/shard_map/ppermute | solution.py:243
  63.9 10.6 %collective-permute-start.20 = (bf16[128,768]{1,0:T(8,128)(2,1)S(1)}, bf16[128,768]{1,0:T(8,128)(2,1)S(1)}, u32[]{:S(2)}, u32[]{:S(2)}) collective-permute-start(bf16[128,768]{1,0:T(8,128)(2,1)S(1)} %get-tuple-element.52), channel_id=1, source_target_pairs={{0,6},{2,4},{4,2},{6,0},{8,14},{10,12},{12,10},{14,8},{16,22},{18,... | collective-permute-start | bytes 589832 | tf_op jit(solution)/shard_map/ppermute | solution.py:243
  70.3 4.2 %copy-start.5 = (bf16[128,768]{1,0:T(8,128)(2,1)}, bf16[128,768]{1,0:T(8,128)(2,1)S(1)}, u32[]{:S(2)}) copy-start(bf16[128,768]{1,0:T(8,128)(2,1)S(1)} %collective-permute-done.18.refs_1_) | copy-start | bytes 589828
  70.3 4.2 %copy-start.6 = (bf16[128,768]{1,0:T(8,128)(2,1)}, bf16[128,768]{1,0:T(8,128)(2,1)S(1)}, u32[]{:S(2)}) copy-start(bf16[128,768]{1,0:T(8,128)(2,1)S(1)} %collective-permute-done.19.refs_2_) | copy-start | bytes 589828
  74.5 0.7 copy-start.7
where the time goes:
time: 78.7 us; the launch traced here: 77.7 us
  Pallas kernels  33.8 us (43%)
  waiting for transfers between devices  17.7 us (22%)
  starting transfers between devices  15.3 us (19%)
  blocking collectives  4.67 us (6%)
  local copies, waits for them, and re-layouts  3.83 us (5%)
  other arithmetic  2.33 us (3%)
    pallas_call x3, Pallas kernels, attend(): pl.pallas_call(functools.partial(attend_kernel, spec), in_specs=[SMEM] *...  27.3 us
    ppermute x21, waiting for transfers between devices, permute(): return lax.ppermute(array, 'ctx', pairs)  17.7 us
    ppermute x21, starting transfers between devices, permute(): return lax.ppermute(array, 'ctx', pairs)  15.3 us
    psum x1, blocking collectives, body(): square = lax.psum(square, 'head')  4.67 us
    pallas_call x2, Pallas kernels, pieces_of(): pl.pallas_call(functools.partial(pieces_kernel, split), in_specs=[SMEM] +...  4.02 us
    unnamed x19, local copies, waits for them, and re-layouts  3.75 us
    pallas_call x1, Pallas kernels, body(): pl.pallas_call(functools.partial(finish_kernel, split), in_specs=[SMEM, S...  2.52 us
    concatenate x2, other arithmetic, body(): jnp.concatenate(got, axis=0).reshape(split * per_device, BLK, HD)  1.71 us
  transfers between devices with their start and end apart: 21, of which 4 were waited for; matrix products, arithmetic and copies ran while one was open for 3% of the time, Pallas kernels for 27%

commit v1 on v0

--- a/solution.py
+++ b/solution.py
@@ -27,8 +27,8 @@
     at = 3
     query_refs = refs[at : at + pieces]
     at += pieces
-    key_refs, value_refs = refs[at : at + len(sources)], refs[at + len(sources) : at + 2 * len(sources)]
-    at += 2 * len(sources)
+    row_refs = refs[at : at + len(sources)]
+    at += len(sources)
     if not first:
         acc_in, stat_in = refs[at : at + 2]
         at += 2
@@ -54,22 +54,21 @@
 
     place, stretch, group = where_ref[0], where_ref[1], where_ref[2]
     count = jnp.int32(0)
-    for index, bits in enumerate(sources):
+    for index, (bits, steps) in enumerate(sources):
         held = jnp.bitwise_xor(group, bits)
-        for step in range(split):
+        for at_step, step in enumerate(steps):
             device = held * split + jnp.bitwise_xor(place, step)
             for block in range(per_device):
                 logical = position_ref[device * per_device + block]
                 live = jnp.bool_(False)
                 for r in range(nr):
-                    low = ranges_ref[(stretch * nr + r) * 2]
-                    high = ranges_ref[(stretch * nr + r) * 2 + 1]
+                    low, high = ranges_ref[r, 0, stretch], ranges_ref[r, 1, stretch]
                     live = live | ((logical >= low) & (logical < high))
 
                 @pl.when(live)
-                def _(count=count, index=index, slot=step * per_device + block):
-                    kept_k[count] = key_refs[index][slot]
-                    kept_v[count] = value_refs[index][slot]
+                def _(count=count, index=index, slot=2 * at_step * per_device + block):
+                    kept_k[count] = row_refs[index][slot]
+                    kept_v[count] = row_refs[index][slot + per_device]
 
                 count = count + live.astype(jnp.int32)
     kept_v[count] = jnp.zeros((BLK, HD), BF16)
@@ -156,20 +155,19 @@
         stat_out[...] = jnp.where(lane < HD // 2, jnp.broadcast_to(top, (width, HD)), acc_ref[:, HD:])
 
 
-def attend(where, ranges, position, q, key_list, value_list, sources, state, last, group_size, per_device):
+def attend(where, ranges, position, q, row_list, sources, state, last, group_size, split, per_device):
     pieces = len(q)
     q_rows = q[0].shape[0]
-    blocks = key_list[0].shape[0]
     width = pieces * q_rows * group_size
-    nr = ranges.shape[0] // (2 * STRETCHES)
+    nr = ranges.shape[0]
     first = state is None
-    most = len(sources) * blocks
-    spec = (tuple(sources), blocks // per_device, per_device, pieces, group_size, first, last, nr)
+    most = sum(rows.shape[0] for rows in row_list) // 2
+    spec = (tuple(sources), split, per_device, pieces, group_size, first, last, nr)
     if last:
         shapes = [jax.ShapeDtypeStruct(q[0].shape, BF16)] * pieces + [jax.ShapeDtypeStruct((8, q_rows), F32)] * pieces
     else:
         shapes = [jax.ShapeDtypeStruct((width, HD), F32)] * 2
-    inputs = 2 * len(sources) + pieces
+    inputs = len(sources) + pieces
     held = [] if first else [pltpu.VMEM((width, HD), F32)] * 2 + [pltpu.SemaphoreType.DMA((2,))]
     return pl.pallas_call(
         functools.partial(attend_kernel, spec),
@@ -187,30 +185,41 @@
         cost_estimate=pl.CostEstimate(
             flops=12 * width * most * BLK * HD, bytes_accessed=4 * width * HD, transcendentals=width * most * BLK
         ),
-    )(where, ranges, position, *q, *key_list, *value_list, *(() if first else state))
-
-
-def pieces_kernel(split, where_ref, *refs):
-    inputs = len(refs) // (split + 1)
-    for index in range(inputs):
-        source = refs[index]
-        width = source.shape[1] // split
-        for step in range(split):
+    )(where, ranges, position, *q, *row_list, *(() if first else state))
+
+
+def pieces_kernel(split, inputs, where_ref, *refs):
+    for step in range(split):
+        row = 0
+        for source in refs[:inputs]:
+            rows, width = source.shape[0], source.shape[1] // split
             start = pl.multiple_of(jnp.bitwise_xor(where_ref[0], step) * width, HD)
-            refs[inputs + index * split + step][...] = source[:, pl.ds(start, width)]
-
-
-def pieces_of(where, split, *arrays):
-    shapes = []
-    for array in arrays:
-        shapes += [jax.ShapeDtypeStruct((array.shape[0], array.shape[1] // split), array.dtype)] * split
-    out = pl.pallas_call(
-        functools.partial(pieces_kernel, split),
-        in_specs=[SMEM] + [VMEM] * len(arrays),
-        out_specs=[VMEM] * len(shapes),
+            refs[len(refs) - split + step][row : row + rows] = source[:, pl.ds(start, width)]
+            row += rows
+
+
+def pieces_of(where, split, arrays, *before):
+    rows = sum(array.shape[0] for array in arrays)
+    shapes = [jax.ShapeDtypeStruct((rows, arrays[0].shape[1] // split), arrays[0].dtype)] * split
+    return pl.pallas_call(
+        functools.partial(pieces_kernel, split, len(arrays)),
+        in_specs=[SMEM] + [VMEM] * len(arrays) + [pl.BlockSpec(memory_space=pl.ANY)] * len(before),
+        out_specs=[VMEM] * split,
         out_shape=shapes,
-    )(where, *arrays)
-    return [out[i * split : (i + 1) * split] for i in range(len(arrays))]
+    )(where, *arrays, *before)
+
+
+def copy_kernel(rows_ref, before_ref, out_ref):
+    out_ref[...] = rows_ref[...]
+
+
+def copy_after(rows, before):
+    return pl.pallas_call(
+        copy_kernel,
+        in_specs=[VMEM, pl.BlockSpec(memory_space=pl.ANY)],
+        out_specs=VMEM,
+        out_shape=jax.ShapeDtypeStruct(rows.shape, rows.dtype),
+    )(rows, before)
 
 
 def finish_kernel(split, where_ref, noise_ref, square_ref, gain_ref, *refs):
@@ -237,7 +246,7 @@
     groups = devices // split
     me = lax.axis_index("ctx")
     here = jnp.stack([lax.rem(me, split), lax.div(me, stretch_devices), lax.div(me, split)]).astype(jnp.int32)
-    ranges_flat = ranges.reshape(-1)
+    ranges_turned = ranges.transpose(1, 2, 0)
 
     def permute(array, pairs):
         return lax.ppermute(array, "ctx", pairs)
@@ -249,24 +258,35 @@
         return [(i, (i // split ^ bits) * split + i % split) for i in range(devices)]
 
     if shared:
-        key_pieces, value_pieces = pieces_of(here, split, keys, values)
-        (query_pieces,) = pieces_of(here, split, queries)
-        own = []
-        for pieces in (key_pieces, value_pieces):
-            got = [pieces[0]] + [permute(pieces[step], within(step)) for step in range(1, split)]
-            own.append(jnp.concatenate(got, axis=0).reshape(split * per_device, BLK, HD))
+        row_pieces = pieces_of(here, split, [keys, values])
+        query_pieces = pieces_of(here, split, [queries])
+        got = [row_pieces[0]] + [permute(row_pieces[step], within(step)) for step in range(1, split)]
+        halves = [range(split // 2), range(split // 2, split)]
+        have = [
+            (0, steps, jnp.concatenate([got[step] for step in steps], axis=0).reshape(-1, BLK, HD)) for steps in halves
+        ]
         q = [query_pieces[0]] + [permute(query_pieces[step], within(step)) for step in range(1, split)]
-        have = [(0, own)]
         reach = groups
         while reach > 1:
-            have += [(bits ^ (reach - 1), [permute(array, between(reach - 1)) for array in rows]) for bits, rows in have]
+            arrived = []
+            for bits, steps, rows in have:
+                if reach == groups and arrived:
+                    rows = copy_after(rows, arrived[-1][2])
+                arrived.append((bits ^ (reach - 1), steps, permute(rows, between(reach - 1))))
+            have += arrived
             reach //= 2
-        phases = [have[:1], have[1:-1], have[-1:]]
+        final = have[-1][0]
+        phases = [
+            [source for source in have if source[0] < 2],
+            [source for source in have if source[0] >= 2 and source[0] != final],
+            [source for source in have if source[0] == final],
+        ]
         state = None
         for index, phase in enumerate(phases):
             state = attend(
-                here, ranges_flat, block_position, q, [rows[0] for _, rows in phase], [rows[1] for _, rows in phase],
-                [bits for bits, _ in phase], state, index == len(phases) - 1, group_size, per_device,
+                here, ranges_turned, block_position, q, [rows for _, _, rows in phase],
+                [(bits, tuple(steps)) for bits, steps, _ in phase], state, index == len(phases) - 1,
+                group_size, split, per_device,
             )
         outs, squares = state[:split], state[split:]
         square = squares[0]
@@ -281,14 +301,14 @@
         for head in range(heads_here):
             columns = slice(head * HD, (head + 1) * HD)
             q = [queries[:, head * group_size * HD : (head + 1) * group_size * HD]]
-            head_keys = key_all[:, columns].reshape(-1, chunk, BLK, HD)
-            head_values = value_all[:, columns].reshape(-1, chunk, BLK, HD)
-            state, chunks = None, head_keys.shape[0]
+            rows = [array[:, columns].reshape(-1, chunk, BLK, HD) for array in (key_all, value_all)]
+            rows = jnp.concatenate(rows, axis=1)
+            state, chunks = None, rows.shape[0]
             for index in range(chunks):
                 numbers = jnp.stack([jnp.int32(0), here[1], jnp.int32(0)])
                 state = attend(
-                    numbers, ranges_flat, block_position, q, [head_keys[index]], [head_values[index]],
-                    [index], state, index == chunks - 1, group_size, chunk,
+                    numbers, ranges_turned, block_position, q, [rows[index]],
+                    [(index, (0,))], state, index == chunks - 1, group_size, 1, chunk,
                 )
             outs.append(state[0])
             square = square + state[1]

time: 78.7 us -> 75.9 us (0.964)
  the two profiles are of different devices: /device:TPU:27 before, /device:TPU:1 now
where the time goes in v1:
time: 75.9 us; the launch traced here: 74.8 us
  Pallas kernels  35 us (46%)
  starting transfers between devices  20.9 us (28%)
  waiting for transfers between devices  8.35 us (11%)
  blocking collectives  4.65 us (6%)
  local copies, waits for them, and re-layouts  4.12 us (5%)
  other arithmetic  1.61 us (2%)
    pallas_call x3, Pallas kernels, attend(): pl.pallas_call(functools.partial(attend_kernel, spec), in_specs=[SMEM] *...  26.8 us
    ppermute x18, starting transfers between devices, permute(): return lax.ppermute(array, 'ctx', pairs)  20.9 us
    ppermute x18, waiting for transfers between devices, permute(): return lax.ppermute(array, 'ctx', pairs)  8.35 us
    psum x1, blocking collectives, body(): square = lax.psum(square, 'head')  4.65 us
    unnamed x28, local copies, waits for them, and re-layouts  4.12 us
    pallas_call x2, Pallas kernels, pieces_of(): pl.pallas_call(functools.partial(pieces_kernel, split, len(arrays)), in_s...  4.02 us
    pallas_call x1, Pallas kernels, body(): pl.pallas_call(functools.partial(finish_kernel, split), in_specs=[SMEM, S...  2.52 us
    pallas_call x1, Pallas kernels, copy_after(): pl.pallas_call(copy_kernel, in_specs=[VMEM, pl.BlockSpec(memory_space=pl....  1.67 us
  transfers between devices with their start and end apart: 18, of which 4 were waited for; matrix products, arithmetic and copies ran while one was open for 1% of the time, Pallas kernels for 31%

profile of v1, /device:TPU:1, one launch (start us, length us, event | category | flops | bytes accessed | tf_op | source)
XLA Modules:
  0.0 74.8 jit_solution(6997539359402484981)
XLA Ops:
  0.0 0.7 pad_add_fusion.where_ref.refs_0_
  0.7 1.9 %shard_map.74 = (bf16[512,128]{1,0:T(8,128)(2,1)}, bf16[512,128]{1,0:T(8,128)(2,1)}, bf16[512,128]{1,0:T(8,128)(2,1)}, bf16[512,128]{1,0:T(8,128)(2,1)}) custom-call(s32[3]{0:T(128)} %pad_add_fusion.where_ref.refs_0_, bf16[256,512]{1,0:T(8,128)(2,1)} %refs_0_.3, bf16[256,512]{1,0:T(8,128)(2,1)} %refs_1_.1), custom_call_target="tpu_custom_call" | custom-call | tf_op jit(solution)/shard_map/pallas_call | solution.py:204
  2.7 2.7 %collective-permute-start.6 = (bf16[512,128]{1,0:T(8,128)(2,1)}, bf16[512,128]{1,0:T(8,128)(2,1)S(1)}, u32[]{:S(2)}, u32[]{:S(2)}) collective-permute-start(bf16[512,128]{1,0:T(8,128)(2,1)} %get-tuple-element.31), channel_id=1, source_target_pairs={{0,4},{2,6},{4,0},{6,2},{8,12},{10,14},{12,8},{14,10},{16,20},{18,... | collective-permute-start | bytes 393224 | tf_op jit(solution)/shard_map/ppermute | solution.py:252
  5.3 0.9 %pad_maximum_fusion = bf16[1024,128]{1,0:T(8,128)(2,1)S(1)} fusion(bf16[512,128]{1,0:T(8,128)(2,1)S(1)} %collective-permute-done.3, bf16[512,128]{1,0:T(8,128)(2,1)} %get-tuple-element.29), kind=kLoop, calls=%fused_computation | loop fusion | flops 524288 | bytes 524288 | tf_op jit(solution)/shard_map/concatenate | solution.py:266
  6.3 3.8 %collective-permute-start.4 = (bf16[8,128,128]{2,1,0:T(8,128)(2,1)S(1)}, bf16[8,128,128]{2,1,0:T(8,128)(2,1)S(1)}, u32[]{:S(2)}, u32[]{:S(2)}) collective-permute-start(bf16[8,128,128]{2,1,0:T(8,128)(2,1)S(1)} %bitcast.8), channel_id=1, source_target_pairs={{0,24},{2,26},{4,28},{6,30},{8,16},{10,18},{12,20},{14,22},{16,8},... | collective-permute-start | bytes 786440 | tf_op jit(solution)/shard_map/ppermute | solution.py:252
  10.1 2.3 %collective-permute-done.7 = bf16[512,128]{1,0:T(8,128)(2,1)S(1)} collective-permute-done((bf16[512,128]{1,0:T(8,128)(2,1)}, bf16[512,128]{1,0:T(8,128)(2,1)S(1)}, u32[]{:S(2)}, u32[]{:S(2)}) %collective-permute-start.7) | collective-permute-done | bytes 131104 | tf_op jit(solution)/shard_map/ppermute | solution.py:252
  12.4 1.6 %collective-permute-start.11 = (bf16[8,128,128]{2,1,0:T(8,128)(2,1)S(1)}, bf16[8,128,128]{2,1,0:T(8,128)(2,1)S(1)}, u32[]{:S(2)}, u32[]{:S(2)}) collective-permute-start(bf16[8,128,128]{2,1,0:T(8,128)(2,1)S(1)} %bitcast.5), channel_id=1, source_target_pairs={{0,8},{2,10},{4,12},{6,14},{8,0},{10,2},{12,4},{14,6},{16,24},{18,... | collective-permute-start | bytes 786440 | tf_op jit(solution)/shard_map/ppermute | solution.py:252
  14.1 2.1 %shard_map.73 = (bf16[128,768]{1,0:T(8,128)(2,1)}, bf16[128,768]{1,0:T(8,128)(2,1)}, bf16[128,768]{1,0:T(8,128)(2,1)}, bf16[128,768]{1,0:T(8,128)(2,1)}) custom-call(s32[3]{0:T(128)} %pad_add_fusion.where_ref.refs_0_, bf16[128,3072]{1,0:T(8,128)(2,1)} %refs_0_.2), custom_call_target="tpu_custom_call" | custom-call | tf_op jit(solution)/shard_map/pallas_call | solution.py:204
  16.2 0.6 collective-permute-start
  16.8 1.3 %collective-permute-start.1 = (bf16[128,768]{1,0:T(8,128)(2,1)}, bf16[128,768]{1,0:T(8,128)(2,1)S(1)}, u32[]{:S(2)}, u32[]{:S(2)}) collective-permute-start(bf16[128,768]{1,0:T(8,128)(2,1)} %get-tuple-element.27), channel_id=1, source_target_pairs={{0,4},{2,6},{4,0},{6,2},{8,12},{10,14},{12,8},{14,10},{16,20},{18,... | collective-permute-start | bytes 589832 | tf_op jit(solution)/shard_map/ppermute | solution.py:252
  18.1 0.5 collective-permute-start.2
  18.8 1.7 %shard_map.75 = bf16[8,128,128]{2,1,0:T(8,128)(2,1)} custom-call(bf16[8,128,128]{2,1,0:T(8,128)(2,1)} %bitcast.6, bf16[8,128,128]{2,1,0:T(8,128)(2,1)} %copy-done.2), custom_call_target="tpu_custom_call" | custom-call | tf_op jit(solution)/shard_map/pallas_call | solution.py:217
  20.5 3.6 %collective-permute-start.8 = (bf16[8,128,128]{2,1,0:T(8,128)(2,1)}, bf16[8,128,128]{2,1,0:T(8,128)(2,1)S(1)}, u32[]{:S(2)}, u32[]{:S(2)}) collective-permute-start(bf16[8,128,128]{2,1,0:T(8,128)(2,1)} %shard_map.75), channel_id=1, source_target_pairs={{0,24},{2,26},{4,28},{6,30},{8,16},{10,18},{12,20},{14,22},{16,8},... | collective-permute-start | bytes 786440 | tf_op jit(solution)/shard_map/ppermute | solution.py:252
  24.1 2.4 %collective-permute-start.5 = (bf16[8,128,128]{2,1,0:T(8,128)(2,1)}, bf16[8,128,128]{2,1,0:T(8,128)(2,1)S(1)}, u32[]{:S(2)}, u32[]{:S(2)}) collective-permute-start(bf16[8,128,128]{2,1,0:T(8,128)(2,1)} %copy-done.2), channel_id=1, source_target_pairs={{0,8},{2,10},{4,12},{6,14},{8,0},{10,2},{12,4},{14,6},{16,24},{18,... | collective-permute-start | bytes 786440 | tf_op jit(solution)/shard_map/ppermute | solution.py:252
  26.5 1.7 %collective-permute-done.2.refs_6_ = bf16[128,768]{1,0:T(8,128)(2,1)S(1)} collective-permute-done((bf16[128,768]{1,0:T(8,128)(2,1)}, bf16[128,768]{1,0:T(8,128)(2,1)S(1)}, u32[]{:S(2)}, u32[]{:S(2)}) %collective-permute-start.2) | collective-permute-done | bytes 196640 | tf_op jit(solution)/shard_map/ppermute | solution.py:252
  28.2 0.9 %copy-done.1 = bf16[1024,128]{1,0:T(8,128)(2,1)S(1)} copy-done((bf16[1024,128]{1,0:T(8,128)(2,1)S(1)}, bf16[1024,128]{1,0:T(8,128)(2,1)}, u32[]{:S(2)}) %copy-start.1) | copy-done | bytes 262168
  29.2 0.9 %copy-done.6 = bf16[128,768]{1,0:T(8,128)(2,1)S(1)} copy-done((bf16[128,768]{1,0:T(8,128)(2,1)S(1)}, bf16[128,768]{1,0:T(8,128)(2,1)}, u32[]{:S(2)}) %copy-start.6) | copy-done | bytes 196632
  30.1 11.2 %shard_map.76 = (f32[3072,128]{1,0:T(8,128)}, f32[3072,128]{1,0:T(8,128)}) custom-call(s32[3]{0:T(128)S(1)} %copy-done.5, s32[2,2,4]{2,1,0:T(2,128)S(1)} %bitcast.11, s32[32]{0:T(128)S(1)} %copy-done.9, bf16[128,768]{1,0:T(8,128)(2,1)S(1)} %copy-done.6, bf16[128,768]{1,0:T(8,128)(2,1)S(1)} %collective-permute-done.refs_4_, ...), custom_call_target="tpu_custom_call" | custom-call | flops 9663676416 | bytes 1572864 | tf_op jit(solution)/shard_map/pallas_call | solution.py:172
  41.4 8.4 %shard_map.77 = (f32[3072,128]{1,0:T(8,128)}, f32[3072,128]{1,0:T(8,128)}) custom-call(s32[3]{0:T(128)S(1)} %copy-done.5, s32[2,2,4]{2,1,0:T(2,128)S(1)} %bitcast.12, s32[32]{0:T(128)S(1)} %copy-done.9, bf16[128,768]{1,0:T(8,128)(2,1)S(1)} %copy-done.6, bf16[128,768]{1,0:T(8,128)(2,1)S(1)} %collective-permute-done.refs_4_, ...), custom_call_target="tpu_custom_call" | custom-call | flops 4831838208 | bytes 1572864 | tf_op jit(solution)/shard_map/pallas_call | solution.py:172
  49.8 0.7 copy-done.13
  50.5 7.2 %shard_map.78 = (bf16[128,768]{1,0:T(8,128)(2,1)S(1)}, bf16[128,768]{1,0:T(8,128)(2,1)S(1)}, bf16[128,768]{1,0:T(8,128)(2,1)S(1)}, bf16[128,768]{1,0:T(8,128)(2,...) custom-call(s32[3]{0:T(128)S(1)} %copy-done.5, ...), custom_call_target="tpu_custom_call" | custom-call | flops 4831838208 | bytes 1572864 | tf_op jit(solution)/shard_map/pallas_call | solution.py:172
  57.7 0.7 copy-done.4
  58.4 0.5 collective-permute-start.12
  58.9 1.2 %collective-permute-start.13 = (f32[8,128]{1,0:T(8,128)S(1)}, f32[8,128]{1,0:T(8,128)S(1)}, u32[]{:S(2)}, u32[]{:S(2)}) collective-permute-start(f32[8,128]{1,0:T(8,128)S(1)} %get-tuple-element.39), channel_id=1, source_target_pairs={{0,4},{2,6},{4,0},{6,2},{8,12},{10,14},{12,8},{14,10},{16,20},{18,... | collective-permute-start | bytes 12296 | tf_op jit(solution)/shard_map/ppermute | solution.py:252
  60.1 0.4 collective-permute-start.14
  60.7 1.2 %collective-permute-start.16 = (bf16[128,768]{1,0:T(8,128)(2,1)S(1)}, bf16[128,768]{1,0:T(8,128)(2,1)S(1)}, u32[]{:S(2)}, u32[]{:S(2)}) collective-permute-start(bf16[128,768]{1,0:T(8,128)(2,1)S(1)} %get-tuple-element.43), channel_id=1, source_target_pairs={{0,4},{2,6},{4,0},{6,2},{8,12},{10,14},{12,8},{14,10},{16,20},{18,... | collective-permute-start | bytes 589832 | tf_op jit(solution)/shard_map/ppermute | solution.py:252
  61.9 0.7 collective-permute-start.17
  62.7 0.4 collective-permute-done.14
  63.1 4.7 %psum.7.square_ref = f32[8,128]{1,0:T(8,128)} all-reduce(f32[8,128]{1,0:T(8,128)S(1)} %add_add_fusion), channel_id=1, replica_groups=mesh['ctx'=16,'head'=2] {'head'}, use_global_device_ids=true, to_apply=%region_0.0 | all-reduce | flops 1024 | bytes 8192 | tf_op jit(solution)/shard_map/psum | solution.py:316
  67.8 3.8 %collective-permute-done.17.refs_3_ = bf16[128,768]{1,0:T(8,128)(2,1)S(1)} collective-permute-done((bf16[128,768]{1,0:T(8,128)(2,1)S(1)}, bf16[128,768]{1,0:T(8,128)(2,1)S(1)}, u32[]{:S(2)}, u32[]{:S(2)}) %collective-permute-start.17) | collective-permute-done | bytes 196640 | tf_op jit(solution)/shard_map/ppermute | solution.py:252
  71.6 0.7 copy-done.12
  72.3 2.5 %shard_map.79 = bf16[128,3072]{1,0:T(8,128)(2,1)} custom-call(s32[3]{0:T(128)} %pad_add_fusion.where_ref.refs_0_, s32[4]{0:T(128)} %noise_ref.1, f32[8,128]{1,0:T(8,128)} %psum.7.square_ref, f32[8,3072]{1,0:T(8,128)} %gain_ref.1, bf16[128,768]{1,0:T(8,128)(2,1)} %copy-done.4, bf16[128,768]{1,0:T(8,128)(2,1)} %copy-done.10, bf16[128,768]{1,0:T(8,128)(2,1)} %copy-done.11, ...), custom_call_target="tpu_custom_call" | custom-call | tf_op jit(solution)/shard_map/pallas_call | solution.py:317
  (44 shorter events, 0.7 us)
Async XLA Ops:
  0.7 27.5 %copy-start.5 = (s32[3]{0:T(128)S(1)}, s32[3]{0:T(128)}, u32[]{:S(2)}) copy-start(s32[3]{0:T(128)} %pad_add_fusion.where_ref.refs_0_) | copy-start | bytes 40
  0.7 27.5 %copy-start.8 = (s32[4,2,2]{0,2,1:T(2,128)S(1)}, s32[4,2,2]{0,2,1:T(2,128)}, u32[]{:S(2)}) copy-start(s32[4,2,2]{0,2,1:T(2,128)} %param.10) | copy-start | bytes 196
  0.7 27.5 %copy-start.9 = (s32[32]{0:T(128)S(1)}, s32[32]{0:T(128)}, u32[]{:S(2)}) copy-start(s32[32]{0:T(128)} %refs_2_.5) | copy-start | bytes 388
  2.6 2.7 %collective-permute-start.3 = (bf16[512,128]{1,0:T(8,128)(2,1)}, bf16[512,128]{1,0:T(8,128)(2,1)S(1)}, u32[]{:S(2)}, u32[]{:S(2)}) collective-permute-start(bf16[512,128]{1,0:T(8,128)(2,1)} %get-tuple-element.30), channel_id=1, source_target_pairs={{0,2},{2,0},{4,6},{6,4},{8,10},{10,8},{12,14},{14,12},{16,18},{18,... | collective-permute-start | bytes 393224 | tf_op jit(solution)/shard_map/ppermute | solution.py:252
  2.7 7.4 %collective-permute-start.6 = (bf16[512,128]{1,0:T(8,128)(2,1)}, bf16[512,128]{1,0:T(8,128)(2,1)S(1)}, u32[]{:S(2)}, u32[]{:S(2)}) collective-permute-start(bf16[512,128]{1,0:T(8,128)(2,1)} %get-tuple-element.31), channel_id=1, source_target_pairs={{0,4},{2,6},{4,0},{6,2},{8,12},{10,14},{12,8},{14,10},{16,20},{18,... | collective-permute-start | bytes 393224 | tf_op jit(solution)/shard_map/ppermute | solution.py:252
  5.3 7.1 %collective-permute-start.7 = (bf16[512,128]{1,0:T(8,128)(2,1)}, bf16[512,128]{1,0:T(8,128)(2,1)S(1)}, u32[]{:S(2)}, u32[]{:S(2)}) collective-permute-start(bf16[512,128]{1,0:T(8,128)(2,1)} %get-tuple-element.32), channel_id=1, source_target_pairs={{0,6},{2,4},{4,2},{6,0},{8,14},{10,12},{12,10},{14,8},{16,22},{18,... | collective-permute-start | bytes 393224 | tf_op jit(solution)/shard_map/ppermute | solution.py:252
  6.3 11.8 %collective-permute-start.4 = (bf16[8,128,128]{2,1,0:T(8,128)(2,1)S(1)}, bf16[8,128,128]{2,1,0:T(8,128)(2,1)S(1)}, u32[]{:S(2)}, u32[]{:S(2)}) collective-permute-start(bf16[8,128,128]{2,1,0:T(8,128)(2,1)S(1)} %bitcast.8), channel_id=1, source_target_pairs={{0,24},{2,26},{4,28},{6,30},{8,16},{10,18},{12,20},{14,22},{16,8},... | collective-permute-start | bytes 786440 | tf_op jit(solution)/shard_map/ppermute | solution.py:252
  12.4 6.2 %copy-start = (bf16[1024,128]{1,0:T(8,128)(2,1)}, bf16[1024,128]{1,0:T(8,128)(2,1)S(1)}, u32[]{:S(2)}) copy-start(bf16[1024,128]{1,0:T(8,128)(2,1)S(1)} %pad_maximum_fusion.1) | copy-start | bytes 786436
  12.4 15.7 %collective-permute-start.11 = (bf16[8,128,128]{2,1,0:T(8,128)(2,1)S(1)}, bf16[8,128,128]{2,1,0:T(8,128)(2,1)S(1)}, u32[]{:S(2)}, u32[]{:S(2)}) collective-permute-start(bf16[8,128,128]{2,1,0:T(8,128)(2,1)S(1)} %bitcast.5), channel_id=1, source_target_pairs={{0,8},{2,10},{4,12},{6,14},{8,0},{10,2},{12,4},{14,6},{16,24},{18,... | collective-permute-start | bytes 786440 | tf_op jit(solution)/shard_map/ppermute | solution.py:252
  14.0 14.2 %collective-permute-start.10 = (bf16[8,128,128]{2,1,0:T(8,128)(2,1)S(1)}, bf16[8,128,128]{2,1,0:T(8,128)(2,1)S(1)}, u32[]{:S(2)}, u32[]{:S(2)}) collective-permute-start(bf16[8,128,128]{2,1,0:T(8,128)(2,1)S(1)} %bitcast.9), channel_id=1, source_target_pairs={{0,8},{2,10},{4,12},{6,14},{8,0},{10,2},{12,4},{14,6},{16,24},{18,... | collective-permute-start | bytes 786440 | tf_op jit(solution)/shard_map/ppermute | solution.py:252
  16.2 4.3 %collective-permute-start = (bf16[128,768]{1,0:T(8,128)(2,1)}, bf16[128,768]{1,0:T(8,128)(2,1)S(1)}, u32[]{:S(2)}, u32[]{:S(2)}) collective-permute-start(bf16[128,768]{1,0:T(8,128)(2,1)} %get-tuple-element.26), channel_id=1, source_target_pairs={{0,2},{2,0},{4,6},{6,4},{8,10},{10,8},{12,14},{14,12},{16,18},{18,... | collective-permute-start | bytes 589832 | tf_op jit(solution)/shard_map/ppermute | solution.py:252
  16.8 7.2 %collective-permute-start.1 = (bf16[128,768]{1,0:T(8,128)(2,1)}, bf16[128,768]{1,0:T(8,128)(2,1)S(1)}, u32[]{:S(2)}, u32[]{:S(2)}) collective-permute-start(bf16[128,768]{1,0:T(8,128)(2,1)} %get-tuple-element.27), channel_id=1, source_target_pairs={{0,4},{2,6},{4,0},{6,2},{8,12},{10,14},{12,8},{14,10},{16,20},{18,... | collective-permute-start | bytes 589832 | tf_op jit(solution)/shard_map/ppermute | solution.py:252
  18.1 0.7 copy-start.2
  18.1 10.0 %collective-permute-start.2 = (bf16[128,768]{1,0:T(8,128)(2,1)}, bf16[128,768]{1,0:T(8,128)(2,1)S(1)}, u32[]{:S(2)}, u32[]{:S(2)}) collective-permute-start(bf16[128,768]{1,0:T(8,128)(2,1)} %get-tuple-element.28), channel_id=1, source_target_pairs={{0,6},{2,4},{4,2},{6,0},{8,14},{10,12},{12,10},{14,8},{16,22},{18,... | collective-permute-start | bytes 589832 | tf_op jit(solution)/shard_map/ppermute | solution.py:252
  20.5 20.9 %collective-permute-start.8 = (bf16[8,128,128]{2,1,0:T(8,128)(2,1)}, bf16[8,128,128]{2,1,0:T(8,128)(2,1)S(1)}, u32[]{:S(2)}, u32[]{:S(2)}) collective-permute-start(bf16[8,128,128]{2,1,0:T(8,128)(2,1)} %shard_map.75), channel_id=1, source_target_pairs={{0,24},{2,26},{4,28},{6,30},{8,16},{10,18},{12,20},{14,22},{16,8},... | collective-permute-start | bytes 786440 | tf_op jit(solution)/shard_map/ppermute | solution.py:252
  24.1 25.7 %collective-permute-start.5 = (bf16[8,128,128]{2,1,0:T(8,128)(2,1)}, bf16[8,128,128]{2,1,0:T(8,128)(2,1)S(1)}, u32[]{:S(2)}, u32[]{:S(2)}) collective-permute-start(bf16[8,128,128]{2,1,0:T(8,128)(2,1)} %copy-done.2), channel_id=1, source_target_pairs={{0,8},{2,10},{4,12},{6,14},{8,0},{10,2},{12,4},{14,6},{16,24},{18,... | collective-permute-start | bytes 786440 | tf_op jit(solution)/shard_map/ppermute | solution.py:252
  28.2 1.0 %copy-start.1 = (bf16[1024,128]{1,0:T(8,128)(2,1)S(1)}, bf16[1024,128]{1,0:T(8,128)(2,1)}, u32[]{:S(2)}) copy-start(bf16[1024,128]{1,0:T(8,128)(2,1)} %copy-done) | copy-start | bytes 786436
  29.2 0.9 %copy-start.6 = (bf16[128,768]{1,0:T(8,128)(2,1)S(1)}, bf16[128,768]{1,0:T(8,128)(2,1)}, u32[]{:S(2)}) copy-start(bf16[128,768]{1,0:T(8,128)(2,1)} %get-tuple-element.25.refs_3_) | copy-start | bytes 589828
  30.1 11.2 %copy-start.3 = (bf16[8,128,128]{2,1,0:T(8,128)(2,1)S(1)}, bf16[8,128,128]{2,1,0:T(8,128)(2,1)}, u32[]{:S(2)}) copy-start(bf16[8,128,128]{2,1,0:T(8,128)(2,1)} %copy-done.2) | copy-start | bytes 786436
  41.3 8.4 %collective-permute-start.9 = (bf16[8,128,128]{2,1,0:T(8,128)(2,1)S(1)}, bf16[8,128,128]{2,1,0:T(8,128)(2,1)S(1)}, u32[]{:S(2)}, u32[]{:S(2)}) collective-permute-start(bf16[8,128,128]{2,1,0:T(8,128)(2,1)S(1)} %collective-permute-done.8.refs_8_), channel_id=1, source_target_pairs={{0,8},{2,10},{4,12},{6,14},{8,0},{10,2},{12,4},{14,6},{16,24},{18,... | collective-permute-start | bytes 786440 | tf_op jit(solution)/shard_map/ppermute | solution.py:252
  41.3 9.1 %copy-start.7 = (bf16[128,768]{1,0:T(8,128)(2,1)S(1)}, bf16[128,768]{1,0:T(8,128)(2,1)}, u32[]{:S(2)}) copy-start(bf16[128,768]{1,0:T(8,128)(2,1)} %get-tuple-element.25.refs_3_) | copy-start | bytes 589828
  49.8 0.7 copy-start.13
  57.7 0.7 copy-start.4
  58.4 3.6 %collective-permute-start.12 = (f32[8,128]{1,0:T(8,128)S(1)}, f32[8,128]{1,0:T(8,128)S(1)}, u32[]{:S(2)}, u32[]{:S(2)}) collective-permute-start(f32[8,128]{1,0:T(8,128)S(1)} %get-tuple-element.38), channel_id=1, source_target_pairs={{0,2},{2,0},{4,6},{6,4},{8,10},{10,8},{12,14},{14,12},{16,18},{18,... | collective-permute-start | bytes 12296 | tf_op jit(solution)/shard_map/ppermute | solution.py:252
  58.9 3.8 %collective-permute-start.13 = (f32[8,128]{1,0:T(8,128)S(1)}, f32[8,128]{1,0:T(8,128)S(1)}, u32[]{:S(2)}, u32[]{:S(2)}) collective-permute-start(f32[8,128]{1,0:T(8,128)S(1)} %get-tuple-element.39), channel_id=1, source_target_pairs={{0,4},{2,6},{4,0},{6,2},{8,12},{10,14},{12,8},{14,10},{16,20},{18,... | collective-permute-start | bytes 12296 | tf_op jit(solution)/shard_map/ppermute | solution.py:252
  60.1 3.0 %collective-permute-start.14 = (f32[8,128]{1,0:T(8,128)S(1)}, f32[8,128]{1,0:T(8,128)S(1)}, u32[]{:S(2)}, u32[]{:S(2)}) collective-permute-start(f32[8,128]{1,0:T(8,128)S(1)} %get-tuple-element.40), channel_id=1, source_target_pairs={{0,6},{2,4},{4,2},{6,0},{8,14},{10,12},{12,10},{14,8},{16,22},{18,... | collective-permute-start | bytes 12296 | tf_op jit(solution)/shard_map/ppermute | solution.py:252
  60.5 7.2 %collective-permute-start.15 = (bf16[128,768]{1,0:T(8,128)(2,1)S(1)}, bf16[128,768]{1,0:T(8,128)(2,1)S(1)}, u32[]{:S(2)}, u32[]{:S(2)}) collective-permute-start(bf16[128,768]{1,0:T(8,128)(2,1)S(1)} %get-tuple-element.42), channel_id=1, source_target_pairs={{0,2},{2,0},{4,6},{6,4},{8,10},{10,8},{12,14},{14,12},{16,18},{18,... | collective-permute-start | bytes 589832 | tf_op jit(solution)/shard_map/ppermute | solution.py:252
  60.7 7.0 %collective-permute-start.16 = (bf16[128,768]{1,0:T(8,128)(2,1)S(1)}, bf16[128,768]{1,0:T(8,128)(2,1)S(1)}, u32[]{:S(2)}, u32[]{:S(2)}) collective-permute-start(bf16[128,768]{1,0:T(8,128)(2,1)S(1)} %get-tuple-element.43), channel_id=1, source_target_pairs={{0,4},{2,6},{4,0},{6,2},{8,12},{10,14},{12,8},{14,10},{16,20},{18,... | collective-permute-start | bytes 589832 | tf_op jit(solution)/shard_map/ppermute | solution.py:252
  61.9 9.6 %collective-permute-start.17 = (bf16[128,768]{1,0:T(8,128)(2,1)S(1)}, bf16[128,768]{1,0:T(8,128)(2,1)S(1)}, u32[]{:S(2)}, u32[]{:S(2)}) collective-permute-start(bf16[128,768]{1,0:T(8,128)(2,1)S(1)} %get-tuple-element.44), channel_id=1, source_target_pairs={{0,6},{2,4},{4,2},{6,0},{8,14},{10,12},{12,10},{14,8},{16,22},{18,... | collective-permute-start | bytes 589832 | tf_op jit(solution)/shard_map/ppermute | solution.py:252
  67.8 3.8 %copy-start.10 = (bf16[128,768]{1,0:T(8,128)(2,1)}, bf16[128,768]{1,0:T(8,128)(2,1)S(1)}, u32[]{:S(2)}) copy-start(bf16[128,768]{1,0:T(8,128)(2,1)S(1)} %collective-permute-done.15.refs_1_) | copy-start | bytes 589828
  67.8 3.8 %copy-start.11 = (bf16[128,768]{1,0:T(8,128)(2,1)}, bf16[128,768]{1,0:T(8,128)(2,1)S(1)}, u32[]{:S(2)}) copy-start(bf16[128,768]{1,0:T(8,128)(2,1)S(1)} %collective-permute-done.16.refs_2_) | copy-start | bytes 589828
  71.6 0.7 copy-start.12
